TPU v7x, 32 devices: a whole 2x2x4 slice. The times are simulated.
32 devices in a mesh: row: 8 (over z, x), col: 4 (over y, core).
Axes of the slice: x: 2, y: 2, z: 4, core: 2. Of those that a mesh axis runs over, the one named last changes fastest.
Arguments:
- currents: bfloat16 [128, 64, 512], P('row', 'col'), may hold values from -6 to 6
- counts: int32 [128, 64], P('row', 'col'), may hold values from 0 to 16
- radiate: bfloat16 [512, 1024], replicated, may hold values from -0.25 to 0.25
- receive: bfloat16 [1024, 512], replicated, may hold values from -0.1875 to 0.1875
- near_blocks: bfloat16 [9, 512, 512], replicated, may hold values from -0.09375 to 0.09375
- translate: float32 [4, 49, 1024], replicated, may hold values from -0.84 to 0.84
- shift: float32 [3, 4, 1024], replicated, may hold values from -3 to 3
Outputs:
- field: bfloat16 [128, 64, 512], P('row', 'col')
Inputs may be any that keep to these rules, and one draw needn't show every extreme that they name: `counts`: atoms present in each leaf box; they occupy its first slots.
All inputs are finite; a program needn't handle non-finite values.
Results may differ from a plain program's by a relative error of at most 0.017.
Values may be sent and summed in bfloat16 or wider, within the bound.
A program may use at most 192 MiB of HBM per device.

v0:
```python
import functools

import jax
import jax.numpy as jnp
import numpy as np
from jax import lax
from jax.experimental import pallas as pl
from jax.experimental.pallas import tpu as pltpu
from jax.sharding import PartitionSpec as P

MESH = pl.DeviceIdType.MESH
F32 = jnp.float32
BF16 = jnp.bfloat16
U = 16
LEVELS = 4
DIRS = [(-1, 0), (1, 0), (0, -1), (0, 1), (-1, -1), (-1, 1), (1, -1), (1, 1)]
SIZE = [32, 32, 32, 32, 16, 16, 16, 16]
OFF = [0, 32, 64, 96, 128, 144, 160, 176]
ROWS = 192
OPP = [1, 0, 3, 2, 7, 6, 5, 4]
SHIFTS = [-2, -1, 0, 1, 2, 3]


def edge(n, step):
    return [0, 1] if step < 0 else ([n - 2, n - 1] if step > 0 else list(range(n)))


def halo(n, step):
    return [-2, -1] if step < 0 else ([n, n + 1] if step > 0 else list(range(n)))


def boxes(d, sizes, pick):
    out = []
    for level, (nx, ny) in enumerate(sizes):
        for x in pick(nx, DIRS[d][0]):
            for y in pick(ny, DIRS[d][1]):
                out.append((level, x, y))
    return out


def message_rows(sizes):
    where = {}
    for d in range(8):
        for k, box in enumerate(boxes(d, sizes, halo)):
            where[box] = OFF[d] + k
    return where


def tables(nx, ny):
    sizes = [(nx >> l, ny >> l) for l in range(LEVELS)]
    own_rows = nx * ny

    def zeros(m, k):
        return np.zeros((m, k), np.float32)

    ex, ey = zeros(own_rows, nx), zeros(own_rows, ny)
    send0 = zeros(ROWS, own_rows)
    perm = zeros(own_rows, own_rows)
    for x in range(nx):
        for y in range(ny):
            ex[x * ny + y, x] = 1
            ey[x * ny + y, y] = 1
            row = (2 * (x % 2) + y % 2) * (own_rows // 4) + (x // 2) * (ny // 2) + y // 2
            perm[row, x * ny + y] = 1
    for d in range(8):
        for k, (_, x, y) in enumerate(boxes(d, sizes[:1], edge)):
            send0[OFF[d] + k, x * ny + y] = 1
    ext_rows = ny + 8
    ext_own, ext_got = zeros((nx + 4) * ext_rows, own_rows), zeros((nx + 4) * ext_rows, ROWS)
    got0 = message_rows(sizes[:1])
    for x in range(-2, nx + 2):
        for y in range(-2, ny + 2):
            row = (x + 2) * ext_rows + y + 3
            if 0 <= x < nx and 0 <= y < ny:
                ext_own[row, x * ny + y] = 1
            else:
                ext_got[row, got0[(0, x, y)]] = 1
    upper = sizes[1:]
    base, total = [], 0
    for a, b in upper:
        base.append(total)
        total += -(-a * b // 8) * 8
    stack = -(-total // 16) * 16

    def own(level, x, y):
        return base[level] + x * upper[level][1] + y

    splits = []
    for level in range(2):
        a, b = upper[level]
        child = -(-a * b // 16) * 16
        quarter = max(8, a * b // 4)
        split = zeros(4 * quarter, child)
        for x in range(a):
            for y in range(b):
                split[(2 * (x % 2) + y % 2) * quarter + (x // 2) * (b // 2) + y // 2, x * b + y] = 1
        splits.append(split)
    send1 = zeros(ROWS, stack)
    for d in range(8):
        for k, (level, x, y) in enumerate(boxes(d, upper, edge)):
            send1[OFF[d] + k, own(level, x, y)] = 1
    got1 = message_rows(upper)
    rows = [max(8, b) for _, b in upper]
    count = sum(6 * (a + 4) * r for (a, _), r in zip(upper, rows))
    up_own, up_got = zeros(count, stack), zeros(count, ROWS)
    at = 0
    for level, (a, b) in enumerate(upper):
        for s in SHIFTS:
            for x in range(-2, a + 2):
                for y in range(b):
                    yy = y + s if s < 3 else (y + 3 if y % 2 == 0 else y - 3)
                    row = at + (x + 2) * rows[level] + y
                    if 0 <= x < a and 0 <= yy < b:
                        up_own[row, own(level, x, yy)] = 1
                    else:
                        up_got[row, got1[(level, x, yy)]] = 1
            at += (a + 4) * rows[level]
    lifts = []
    for level in range(LEVELS - 1):
        a, b = sizes[level]
        r, rp = max(8, b), max(8, b // 2)
        lift = zeros(a * r, (a // 2) * rp)
        for x in range(a):
            for y in range(b):
                lift[x * r + y, (x // 2) * rp + y // 2] = 1
        lifts.append(np.concatenate([lift] * 3, axis=1))
    out = dict(ex=ex, ey=ey, send0=send0, perm=perm, ext_own=ext_own, ext_got=ext_got, split1=splits[0],
               split2=splits[1], send1=send1, up_own=up_own, up_got=up_got, lift0=lifts[0], lift1=lifts[1], lift2=lifts[2])
    return out, sizes


def dot(a, b):
    return jnp.dot(a, b, preferred_element_type=F32)


def body(names, sizes, *refs):
    n_in = len(names)
    hbm = dict(zip(names, refs[:n_in]))
    out_ref = refs[n_in]
    vm = dict(zip(names, refs[n_in + 1 : 2 * n_in + 1]))
    (x_own, cs, cr, gp, lown, ls, lr, e0, f0, ns, ps0, psl, inc0, inc1, inc2, inc3, lift0, lift1, lift2, near, cnt,
     in_sem, s_send, s_recv) = refs[2 * n_in + 1 :]
    nx, ny = sizes[0]
    own = nx * ny
    w = x_own.shape[1]
    feat = gp.shape[1]
    half = feat // 2
    tiles = half // 128
    row, col = lax.axis_index("row"), lax.axis_index("col")
    n_row, n_col = lax.axis_size("row"), lax.axis_size("col")

    loads = {name: pltpu.make_async_copy(hbm[name], vm[name], in_sem.at[k]) for k, name in enumerate(names)}
    for name in names:
        loads[name].start()

    cr[...] = jnp.zeros_like(cr)
    lr[...] = jnp.zeros_like(lr)

    there, ident = [], []
    for dr, dc in DIRS:
        r, c = row + dr, col + dc
        ok = (r >= 0) & (r < n_row) & (c >= 0) & (c < n_col)
        there.append(ok)
        ident.append((r, c))
    barrier = pltpu.get_barrier_semaphore()
    total = jnp.int32(0)
    for d in range(8):
        total = total + there[d].astype(jnp.int32)

        @pl.when(there[d])
        def _():
            pl.semaphore_signal(barrier, inc=1, device_id=ident[d], device_id_type=MESH)

    def copy(phase, src, dst, d, recv):
        o = OPP[d]
        slot = d if recv else o
        return pltpu.make_async_remote_copy(
            src_ref=src.at[pl.ds(OFF[d], SIZE[d])],
            dst_ref=dst.at[pl.ds(OFF[slot], SIZE[d])],
            send_sem=s_send.at[phase, d],
            recv_sem=s_recv.at[phase, slot],
            device_id=ident[d],
            device_id_type=MESH,
        )

    def each(act):
        for d in range(8):
            @pl.when(there[d])
            def _():
                act(d)

    for name in ("counts", "ex", "ey", "currents", "send0"):
        loads[name].wait()
    per_row = dot(vm["ex"][...], vm["counts"][...].astype(F32).astype(BF16)) * vm["ey"][...].astype(F32)
    cnt[...] = dot(per_row.astype(BF16), jnp.ones((ny, w), BF16))
    slot_of = (lax.broadcasted_iota(jnp.int32, (own, w), 1) // (2 * U)).astype(F32)
    occupied = slot_of < cnt[...]
    flat = vm["currents"][...].reshape(own, w)
    x_own[...] = jnp.where(occupied, flat.astype(F32), 0.0).astype(BF16)
    cs[...] = dot(vm["send0"][...], x_own[...]).astype(BF16)
    pl.semaphore_wait(barrier, total)
    each(lambda d: copy(0, cs, cr, d, False).start())

    loads["perm"].wait()
    loads["radiate"].wait()
    loads["shift"].wait()
    mixed = dot(vm["perm"][...], x_own[...]).astype(BF16)
    gp[...] = dot(mixed, vm["radiate"][...]).astype(BF16).astype(F32)
    shift = vm["shift"]
    quarter = own // 4

    def gather_up(source, level, rows):
        res, ims = [], []
        for t in range(tiles):
            lr_, li_ = slice(t * 128, t * 128 + 128), slice(half + t * 128, half + t * 128 + 128)
            re = jnp.zeros((rows, 128), F32)
            im = jnp.zeros((rows, 128), F32)
            for ab in range(4):
                tr, ti = shift[level, ab : ab + 1, lr_], shift[level, ab : ab + 1, li_]
                pr, pi = source[ab * rows : (ab + 1) * rows, lr_], source[ab * rows : (ab + 1) * rows, li_]
                re = re + (tr * pr - ti * pi)
                im = im + (tr * pi + ti * pr)
            res.append(re)
            ims.append(im)
        return jnp.concatenate(res + ims, axis=1)

    p1 = gather_up(gp, 0, quarter).astype(BF16)
    lown[0:quarter] = p1
    loads["split1"].wait()
    loads["split2"].wait()
    loads["send1"].wait()
    q2 = quarter // 4
    p2 = gather_up(dot(vm["split1"][...], p1), 1, q2).astype(BF16)
    lown[quarter : quarter + q2] = p2
    p3 = gather_up(dot(vm["split2"][...], p2), 2, 8)
    tail = lown.shape[0] - quarter - q2
    lown[quarter + q2 :] = jnp.concatenate([p3, jnp.zeros((tail - 8, feat), F32)], axis=0).astype(BF16)
    ls[...] = dot(vm["send1"][...], lown[...]).astype(BF16)
    each(lambda d: copy(1, ls, lr, d, False).start())

    loads["ext_own"].wait()
    loads["ext_got"].wait()
    each(lambda d: copy(0, cs, cr, d, True).wait_recv())
    ext = dot(vm["ext_own"][...], x_own[...]) + dot(vm["ext_got"][...], cr[...])
    ext_rows = ny + 8
    f0[...] = ext.reshape(nx + 4, ext_rows, w)
    step_rows = 4 * ext_rows

    def radiate_some(k, _):
        some = f0[pl.ds(k * 4, 4)].reshape(step_rows, w).astype(BF16)
        e0[pl.ds(k * 4, 4)] = dot(some, vm["radiate"][...]).astype(BF16).astype(F32).reshape(4, ext_rows, feat)
        return 0

    lax.fori_loop(0, (nx + 4) // 4, radiate_some, 0)

    even16 = (lax.broadcasted_iota(jnp.int32, (1, ny, 128), 1) % 2) == 0
    pairs = nx // 2 + 2

    def shifted(k, _):
        for c in range(feat // 128):
            lanes = slice(c * 128, c * 128 + 128)
            for par in range(2):
                x = k * 2 + par
                for n, s in enumerate(SHIFTS):
                    v = e0[pl.ds(x, 1), 3 + s : 3 + s + ny, lanes]
                    if s == 3:
                        v = jnp.where(even16, v, e0[pl.ds(x, 1), 0:ny, lanes])
                    ps0[pl.ds(n * pairs + k, 1), par, :, lanes] = v
        return 0

    lax.fori_loop(0, pairs, shifted, 0)

    for n in range(3):
        ns[n] = f0[1 : nx + 3, 2 + n : 2 + n + ny, :].astype(BF16)
    loads["near_blocks"].wait()
    for k in range(9):
        dx, dy = k // 3, k % 3
        part = dot(ns[dy, dx : dx + nx].reshape(own, w), vm["near_blocks"][k])
        near[...] = part if k == 0 else near[...] + part

    loads["up_own"].wait()
    loads["up_got"].wait()
    loads["translate"].wait()
    each(lambda d: copy(1, ls, lr, d, True).wait_recv())
    blocks = psl.shape[0] // 6

    def upper_some(k, _):
        rows = pl.ds(pl.multiple_of(k * 96, 96), 96)
        v = dot(vm["up_own"][rows, :], lown[...]) + dot(vm["up_got"][rows, :], lr[...])
        psl[pl.ds(k * 6, 6)] = v.reshape(6, 2, 8, feat)
        return 0

    lax.fori_loop(0, blocks, upper_some, 0)

    translate = vm["translate"]

    def far(level, src, base, inc, lifted):
        rows = src.shape[2]
        n_pairs = sizes[level][0] // 2
        npair = n_pairs + 2
        ni = min(4, n_pairs)
        even = (lax.broadcasted_iota(jnp.int32, (rows, 128), 0) % 2) == 0

        def step(it, _):
            t, h = lax.rem(it, tiles), lax.div(it, tiles)
            rl = pl.ds(pl.multiple_of(t * 128, 128), 128)
            il = pl.ds(pl.multiple_of(half + t * 128, 128), 128)
            for a in range(2):
                re = jnp.zeros((ni, rows, 128), F32)
                im = jnp.zeros((ni, rows, 128), F32)
                for e in range(6):
                    dx = e - 2 - a
                    for n, s in enumerate(SHIFTS):
                        if max(abs(dx), abs(s)) < 2:
                            continue
                        k = (dx + 3) * 7 + s + 3
                        tr, ti = translate[level, k : k + 1, rl], translate[level, k : k + 1, il]
                        if s == 3:
                            m = (dx + 3) * 7
                            tr = jnp.where(even, tr, translate[level, m : m + 1, rl])
                            ti = jnp.where(even, ti, translate[level, m : m + 1, il])
                        at = pl.ds(base + n * npair + e // 2 + h * ni, ni)
                        pr, pi = src[at, e % 2, :, rl], src[at, e % 2, :, il]
                        re = re + (tr * pr - ti * pi)
                        im = im + (tr * pi + ti * pr)
                at = pl.ds(h * ni, ni)
                if lifted is not None:
                    tr = jnp.where(even, shift[level, 2 * a : 2 * a + 1, rl], shift[level, 2 * a + 1 : 2 * a + 2, rl])
                    ti = jnp.where(even, shift[level, 2 * a : 2 * a + 1, il], shift[level, 2 * a + 1 : 2 * a + 2, il])
                    pr, pi = lifted[at, a, :, rl], lifted[at, a, :, il]
                    re = re + (tr * pr + ti * pi)
                    im = im + (tr * pi - ti * pr)
                inc[at, a, :, rl] = re.astype(inc.dtype)
                inc[at, a, :, il] = im.astype(inc.dtype)
            return 0

        lax.fori_loop(0, tiles * (n_pairs // ni), step, 0)

    def lift(name, inc, dst):
        loads[name].wait()
        v = inc[...].reshape(-1, feat)
        hi = v.astype(BF16)
        rest = v - hi.astype(F32)
        mid = rest.astype(BF16)
        low = (rest - mid.astype(F32)).astype(BF16)
        dst[...] = dot(vm[name][...], jnp.concatenate([hi, mid, low], axis=0)).reshape(dst.shape)

    bases, at = [], 0
    for a, _ in sizes[1:]:
        bases.append(at)
        at += 6 * (a // 2 + 2)
    far(3, psl, bases[2], inc3, None)
    lift("lift2", inc3, lift2)
    far(2, psl, bases[1], inc2, lift2)
    lift("lift1", inc2, lift1)
    far(1, psl, bases[0], inc1, lift1)
    lift("lift0", inc1, lift0)
    far(0, ps0, 0, inc0, lift0)

    loads["receive"].wait()
    field = near[...] + dot(inc0[...].reshape(own, feat), vm["receive"][...])
    out_ref[...] = jnp.where(slot_of < cnt[...], field, 0.0).astype(BF16).reshape(nx, ny, w)

    each(lambda d: copy(0, cs, cr, d, False).wait_send())
    each(lambda d: copy(1, ls, lr, d, False).wait_send())


ORDER = ["counts", "ex", "ey", "currents", "send0", "perm", "radiate", "shift", "split1", "split2", "send1", "ext_own",
         "ext_got", "near_blocks", "up_own", "up_got", "translate", "lift2", "lift1", "lift0", "receive"]


def shards(currents, counts, radiate, receive, near_blocks, translate, shift):
    nx, ny, w = currents.shape
    feat = radiate.shape[1]
    consts, sizes = tables(nx, ny)
    ops = {k: jnp.asarray(v, BF16) for k, v in consts.items()}
    ops.update(currents=currents, counts=counts, radiate=radiate, receive=receive, near_blocks=near_blocks,
               translate=translate, shift=shift)
    args = [ops[k] for k in ORDER]
    own = nx * ny
    stack = consts["send1"].shape[1]
    rows = [max(8, b) for _, b in sizes]

    def level_buffer(level, dtype):
        return pltpu.VMEM((sizes[level][0] // 2, 2, rows[level], feat), dtype)

    scratch = [pltpu.VMEM(a.shape, a.dtype) for a in args]
    scratch += [
        pltpu.VMEM((own, w), BF16),
        pltpu.VMEM((ROWS, w), BF16),
        pltpu.VMEM((ROWS, w), BF16),
        pltpu.VMEM((own, feat), F32),
        pltpu.VMEM((stack, feat), BF16),
        pltpu.VMEM((ROWS, feat), BF16),
        pltpu.VMEM((ROWS, feat), BF16),
        pltpu.VMEM((nx + 4, ny + 8, feat), F32),
        pltpu.VMEM((nx + 4, ny + 8, w), F32),
        pltpu.VMEM((3, nx + 2, ny, w), BF16),
        pltpu.VMEM((6 * (nx // 2 + 2), 2, ny, feat), F32),
        pltpu.VMEM((consts["up_own"].shape[0] // 16, 2, 8, feat), F32),
        level_buffer(0, BF16), level_buffer(1, F32), level_buffer(2, F32), level_buffer(3, F32),
        level_buffer(0, F32), level_buffer(1, F32), level_buffer(2, F32),
        pltpu.VMEM((own, w), F32),
        pltpu.VMEM((own, w), F32),
        pltpu.SemaphoreType.DMA((len(args),)),
        pltpu.SemaphoreType.DMA((2, 8)),
        pltpu.SemaphoreType.DMA((2, 8)),
    ]
    return pl.pallas_call(
        functools.partial(body, ORDER, sizes),
        out_shape=jax.ShapeDtypeStruct(currents.shape, BF16),
        in_specs=[pl.BlockSpec(memory_space=pl.ANY)] * len(args),
        out_specs=pl.BlockSpec(memory_space=pltpu.VMEM),
        scratch_shapes=scratch,
        compiler_params=pltpu.CompilerParams(
            collective_id=0, has_side_effects=True, vmem_limit_bytes=58 * 1024 * 1024
        ),
        cost_estimate=pl.CostEstimate(flops=3_000_000_000, bytes_accessed=12_000_000, transcendentals=0),
    )(*args)


def solution(mesh):
    return jax.shard_map(
        shards,
        mesh=mesh,
        in_specs=(P("row", "col", None), P("row", "col"), P(), P(), P(), P(), P()),
        out_specs=P("row", "col", None),
        check_vma=False,
    )
```

profile of v0, /device:TPU:25, one launch (start us, length us, event | category | flops | bytes accessed | tf_op | source)
XLA Modules:
  0.0 33.6 jit_solution(14479313086164441563)
XLA Ops:
  0.0 2.5 %copy.22.refs_16_ = f32[4,49,1024]{2,1,0:T(8,128)} copy(f32[4,49,1024]{2,0,1:T(4,128)} %param.26) | data formatting | bytes 1605632 | tf_op args[5]
  2.5 29.4 %shard_map.199 = bf16[16,16,512]{2,1,0:T(8,128)(2,1)} custom-call(s32[16,16]{1,0:T(8,128)} %refs_0_.1, bf16[256,16]{1,0:T(8,128)(2,1)} %constant.28.clone.refs_1_, bf16[256,16]{1,0:T(8,128)(2,1)} %constant.29.clone.refs_2_, bf16[16,16,512]{2,1,0:T(8,128)(2,1)} %refs_3_.1, bf16[192,256]{1,0:T(8,128)(2,1)} %constant.30.clone.refs_4_, ...), custom_call_target="tpu_custom_call" | custom-call | flops 3000000000 | bytes 12000000 | tf_op jit(solution)/shard_map/pallas_call | solution.py:409
  31.9 1.7 %copy.24 = bf16[16,16,512]{2,1,0:T(8,128)(2,1)} copy(bf16[16,16,512]{2,1,0:T(8,128)(2,1)} %shard_map.199) | data formatting | bytes 524288
where the time goes:
time: 33.8 us; the launch traced here: 33.6 us
  Pallas kernels  29.4 us (87%)
  local copies, waits for them, and re-layouts  4.21 us (12%)
    pallas_call x1, Pallas kernels, shards(): pl.pallas_call(functools.partial(body, ORDER, sizes), out_shape=jax.Shape...  29.4 us
    unnamed x2, local copies, waits for them, and re-layouts  4.21 us

commit v1 on v0

--- a/solution.py
+++ b/solution.py
@@ -138,7 +138,7 @@
     hbm = dict(zip(names, refs[:n_in]))
     out_ref = refs[n_in]
     vm = dict(zip(names, refs[n_in + 1 : 2 * n_in + 1]))
-    (x_own, cs, cr, gp, lown, ls, lr, e0, f0, ns, ps0, psl, inc0, inc1, inc2, inc3, lift0, lift1, lift2, near, cnt,
+    (x_own, cs, cr, gp, lown, ls, lr, e0, f0, ns, ps0, psl, far0, inc0, inc1, inc2, inc3, lift0, lift1, lift2, near, cnt,
      in_sem, s_send, s_recv) = refs[2 * n_in + 1 :]
     nx, ny = sizes[0]
     own = nx * ny
@@ -150,9 +150,6 @@
     n_row, n_col = lax.axis_size("row"), lax.axis_size("col")
 
     loads = {name: pltpu.make_async_copy(hbm[name], vm[name], in_sem.at[k]) for k, name in enumerate(names)}
-    for name in names:
-        loads[name].start()
-
     cr[...] = jnp.zeros_like(cr)
     lr[...] = jnp.zeros_like(lr)
 
@@ -170,6 +167,9 @@
         @pl.when(there[d])
         def _():
             pl.semaphore_signal(barrier, inc=1, device_id=ident[d], device_id_type=MESH)
+
+    for name in names[:EARLY]:
+        loads[name].start()
 
     def copy(phase, src, dst, d, recv):
         o = OPP[d]
@@ -200,6 +200,8 @@
     cs[...] = dot(vm["send0"][...], x_own[...]).astype(BF16)
     pl.semaphore_wait(barrier, total)
     each(lambda d: copy(0, cs, cr, d, False).start())
+    for name in names[EARLY:]:
+        loads[name].start()
 
     loads["perm"].wait()
     loads["radiate"].wait()
@@ -273,25 +275,10 @@
     for n in range(3):
         ns[n] = f0[1 : nx + 3, 2 + n : 2 + n + ny, :].astype(BF16)
     loads["near_blocks"].wait()
-    for k in range(9):
-        dx, dy = k // 3, k % 3
-        part = dot(ns[dy, dx : dx + nx].reshape(own, w), vm["near_blocks"][k])
-        near[...] = part if k == 0 else near[...] + part
-
-    loads["up_own"].wait()
-    loads["up_got"].wait()
+    views = [ns[k % 3, k // 3 : k // 3 + nx].reshape(own, w) for k in range(9)]
+    near[...] = dot(jnp.concatenate(views, axis=1), vm["near_blocks"][...].reshape(9 * w, w))
+
     loads["translate"].wait()
-    each(lambda d: copy(1, ls, lr, d, True).wait_recv())
-    blocks = psl.shape[0] // 6
-
-    def upper_some(k, _):
-        rows = pl.ds(pl.multiple_of(k * 96, 96), 96)
-        v = dot(vm["up_own"][rows, :], lown[...]) + dot(vm["up_got"][rows, :], lr[...])
-        psl[pl.ds(k * 6, 6)] = v.reshape(6, 2, 8, feat)
-        return 0
-
-    lax.fori_loop(0, blocks, upper_some, 0)
-
     translate = vm["translate"]
 
     def far(level, src, base, inc, lifted):
@@ -314,11 +301,11 @@
                         if max(abs(dx), abs(s)) < 2:
                             continue
                         k = (dx + 3) * 7 + s + 3
-                        tr, ti = translate[level, k : k + 1, rl], translate[level, k : k + 1, il]
+                        tr, ti = translate[k, level : level + 1, rl], translate[k, level : level + 1, il]
                         if s == 3:
                             m = (dx + 3) * 7
-                            tr = jnp.where(even, tr, translate[level, m : m + 1, rl])
-                            ti = jnp.where(even, ti, translate[level, m : m + 1, il])
+                            tr = jnp.where(even, tr, translate[m, level : level + 1, rl])
+                            ti = jnp.where(even, ti, translate[m, level : level + 1, il])
                         at = pl.ds(base + n * npair + e // 2 + h * ni, ni)
                         pr, pi = src[at, e % 2, :, rl], src[at, e % 2, :, il]
                         re = re + (tr * pr - ti * pi)
@@ -345,6 +332,21 @@
         low = (rest - mid.astype(F32)).astype(BF16)
         dst[...] = dot(vm[name][...], jnp.concatenate([hi, mid, low], axis=0)).reshape(dst.shape)
 
+    far(0, ps0, 0, far0, None)
+
+    loads["up_own"].wait()
+    loads["up_got"].wait()
+    each(lambda d: copy(1, ls, lr, d, True).wait_recv())
+    blocks = psl.shape[0] // 6
+
+    def upper_some(k, _):
+        rows = pl.ds(pl.multiple_of(k * 96, 96), 96)
+        v = dot(vm["up_own"][rows, :], lown[...]) + dot(vm["up_got"][rows, :], lr[...])
+        psl[pl.ds(k * 6, 6)] = v.reshape(6, 2, 8, feat)
+        return 0
+
+    lax.fori_loop(0, blocks, upper_some, 0)
+
     bases, at = [], 0
     for a, _ in sizes[1:]:
         bases.append(at)
@@ -355,16 +357,31 @@
     lift("lift1", inc2, lift1)
     far(1, psl, bases[0], inc1, lift1)
     lift("lift0", inc1, lift0)
-    far(0, ps0, 0, inc0, lift0)
+
+    even = (lax.broadcasted_iota(jnp.int32, (ny, 128), 0) % 2) == 0
+
+    def from_parents(t, _):
+        rl = pl.ds(pl.multiple_of(t * 128, 128), 128)
+        il = pl.ds(pl.multiple_of(half + t * 128, 128), 128)
+        for a in range(2):
+            tr = jnp.where(even, shift[0, 2 * a : 2 * a + 1, rl], shift[0, 2 * a + 1 : 2 * a + 2, rl])
+            ti = jnp.where(even, shift[0, 2 * a : 2 * a + 1, il], shift[0, 2 * a + 1 : 2 * a + 2, il])
+            pr, pi = lift0[:, a, :, rl], lift0[:, a, :, il]
+            inc0[:, a, :, rl] = (far0[:, a, :, rl] + (tr * pr + ti * pi)).astype(BF16)
+            inc0[:, a, :, il] = (far0[:, a, :, il] + (tr * pi - ti * pr)).astype(BF16)
+        return 0
+
+    lax.fori_loop(0, tiles, from_parents, 0)
 
     loads["receive"].wait()
     field = near[...] + dot(inc0[...].reshape(own, feat), vm["receive"][...])
-    out_ref[...] = jnp.where(slot_of < cnt[...], field, 0.0).astype(BF16).reshape(nx, ny, w)
+    out_ref[...] = jnp.where(slot_of < cnt[...], field, 0.0).reshape(nx, ny, w)
 
     each(lambda d: copy(0, cs, cr, d, False).wait_send())
     each(lambda d: copy(1, ls, lr, d, False).wait_send())
 
 
+EARLY = 11
 ORDER = ["counts", "ex", "ey", "currents", "send0", "perm", "radiate", "shift", "split1", "split2", "send1", "ext_own",
          "ext_got", "near_blocks", "up_own", "up_got", "translate", "lift2", "lift1", "lift0", "receive"]
 
@@ -375,7 +392,7 @@
     consts, sizes = tables(nx, ny)
     ops = {k: jnp.asarray(v, BF16) for k, v in consts.items()}
     ops.update(currents=currents, counts=counts, radiate=radiate, receive=receive, near_blocks=near_blocks,
-               translate=translate, shift=shift)
+               translate=jnp.transpose(translate, (1, 0, 2)), shift=shift)
     args = [ops[k] for k in ORDER]
     own = nx * ny
     stack = consts["send1"].shape[1]
@@ -398,7 +415,7 @@
         pltpu.VMEM((3, nx + 2, ny, w), BF16),
         pltpu.VMEM((6 * (nx // 2 + 2), 2, ny, feat), F32),
         pltpu.VMEM((consts["up_own"].shape[0] // 16, 2, 8, feat), F32),
-        level_buffer(0, BF16), level_buffer(1, F32), level_buffer(2, F32), level_buffer(3, F32),
+        level_buffer(0, F32), level_buffer(0, BF16), level_buffer(1, F32), level_buffer(2, F32), level_buffer(3, F32),
         level_buffer(0, F32), level_buffer(1, F32), level_buffer(2, F32),
         pltpu.VMEM((own, w), F32),
         pltpu.VMEM((own, w), F32),
@@ -408,7 +425,7 @@
     ]
     return pl.pallas_call(
         functools.partial(body, ORDER, sizes),
-        out_shape=jax.ShapeDtypeStruct(currents.shape, BF16),
+        out_shape=jax.ShapeDtypeStruct(currents.shape, F32),
         in_specs=[pl.BlockSpec(memory_space=pl.ANY)] * len(args),
         out_specs=pl.BlockSpec(memory_space=pltpu.VMEM),
         scratch_shapes=scratch,
@@ -416,7 +433,7 @@
             collective_id=0, has_side_effects=True, vmem_limit_bytes=58 * 1024 * 1024
         ),
         cost_estimate=pl.CostEstimate(flops=3_000_000_000, bytes_accessed=12_000_000, transcendentals=0),
-    )(*args)
+    )(*args).astype(BF16)
 
 
 def solution(mesh):

time: 33.8 us -> 31 us (0.917)
  local copies, waits for them, and re-layouts: 4.21 us -> 0 us
  other arithmetic: 0 us -> 1.78 us
  Pallas kernels: 29.4 us -> 29 us
    unnamed x2 -> x0, local copies, waits for them, and re-layouts: 4.21 us -> none
    convert_element_type x0 -> x1, other arithmetic: none -> 1.78 us  [shards(): return pl.pallas_call(functools.partial(body, ORDER, sizes), out_shape=ja...]
where the time goes in v1:
time: 31 us; the launch traced here: 30.8 us
  Pallas kernels  29 us (94%)
  other arithmetic  1.78 us (6%)
    pallas_call x1, Pallas kernels, shards(): pl.pallas_call(functools.partial(body, ORDER, sizes), out_shape=jax.Shape...  29 us
    convert_element_type x1, other arithmetic, shards(): return pl.pallas_call(functools.partial(body, ORDER, sizes), out_shape=ja...  1.78 us

profile of v1, /device:TPU:25, one launch (start us, length us, event | category | flops | bytes accessed | tf_op | source)
XLA Modules:
  0.0 30.8 jit_solution(1769418312335236225)
XLA Ops:
  0.0 29.0 %shard_map.199 = f32[16,16,512]{2,1,0:T(8,128)} custom-call(s32[16,16]{1,0:T(8,128)} %refs_0_.1, bf16[256,16]{1,0:T(8,128)(2,1)} %constant.28.clone.refs_1_, bf16[256,16]{1,0:T(8,128)(2,1)} %constant.29.clone.refs_2_, bf16[16,16,512]{2,1,0:T(8,128)(2,1)} %refs_3_.1, bf16[192,256]{1,0:T(8,128)(2,1)} %constant.30.clone.refs_4_, ...), custom_call_target="tpu_custom_call" | custom-call | flops 3000000000 | bytes 12000000 | tf_op jit(solution)/shard_map/pallas_call | solution.py:426
  29.0 1.8 %convert_element_type.3 = bf16[16,16,512]{2,1,0:T(8,128)(2,1)} convert(f32[16,16,512]{2,1,0:T(8,128)} %shard_map.199) | non-fusion elementwise | flops 131072 | bytes 786432 | tf_op jit(solution)/shard_map/convert_element_type | solution.py:436

commit v2 on v1

--- a/solution.py
+++ b/solution.py
@@ -245,15 +245,13 @@
     each(lambda d: copy(0, cs, cr, d, True).wait_recv())
     ext = dot(vm["ext_own"][...], x_own[...]) + dot(vm["ext_got"][...], cr[...])
     ext_rows = ny + 8
-    f0[...] = ext.reshape(nx + 4, ext_rows, w)
-    step_rows = 4 * ext_rows
-
-    def radiate_some(k, _):
-        some = f0[pl.ds(k * 4, 4)].reshape(step_rows, w).astype(BF16)
-        e0[pl.ds(k * 4, 4)] = dot(some, vm["radiate"][...]).astype(BF16).astype(F32).reshape(4, ext_rows, feat)
-        return 0
-
-    lax.fori_loop(0, (nx + 4) // 4, radiate_some, 0)
+    for c in range(w // 128):
+        f0[c] = ext[:, c * 128 : c * 128 + 128].reshape(nx + 4, ext_rows, 128)
+    ext = ext.astype(BF16)
+    for c in range(0, feat // 128, 2):
+        pat = dot(ext, vm["radiate"][:, c * 128 : c * 128 + 256]).astype(BF16).astype(F32)
+        e0[c] = pat[:, :128].reshape(nx + 4, ext_rows, 128)
+        e0[c + 1] = pat[:, 128:].reshape(nx + 4, ext_rows, 128)
 
     even16 = (lax.broadcasted_iota(jnp.int32, (1, ny, 128), 1) % 2) == 0
     pairs = nx // 2 + 2
@@ -264,16 +262,17 @@
             for par in range(2):
                 x = k * 2 + par
                 for n, s in enumerate(SHIFTS):
-                    v = e0[pl.ds(x, 1), 3 + s : 3 + s + ny, lanes]
+                    v = e0[c, pl.ds(x, 1), 3 + s : 3 + s + ny, :]
                     if s == 3:
-                        v = jnp.where(even16, v, e0[pl.ds(x, 1), 0:ny, lanes])
+                        v = jnp.where(even16, v, e0[c, pl.ds(x, 1), 0:ny, :])
                     ps0[pl.ds(n * pairs + k, 1), par, :, lanes] = v
         return 0
 
     lax.fori_loop(0, pairs, shifted, 0)
 
     for n in range(3):
-        ns[n] = f0[1 : nx + 3, 2 + n : 2 + n + ny, :].astype(BF16)
+        for c in range(w // 128):
+            ns[n, :, :, c * 128 : c * 128 + 128] = f0[c, 1 : nx + 3, 2 + n : 2 + n + ny, :].astype(BF16)
     loads["near_blocks"].wait()
     views = [ns[k % 3, k // 3 : k // 3 + nx].reshape(own, w) for k in range(9)]
     near[...] = dot(jnp.concatenate(views, axis=1), vm["near_blocks"][...].reshape(9 * w, w))
@@ -337,15 +336,9 @@
     loads["up_own"].wait()
     loads["up_got"].wait()
     each(lambda d: copy(1, ls, lr, d, True).wait_recv())
-    blocks = psl.shape[0] // 6
-
-    def upper_some(k, _):
-        rows = pl.ds(pl.multiple_of(k * 96, 96), 96)
-        v = dot(vm["up_own"][rows, :], lown[...]) + dot(vm["up_got"][rows, :], lr[...])
-        psl[pl.ds(k * 6, 6)] = v.reshape(6, 2, 8, feat)
-        return 0
-
-    lax.fori_loop(0, blocks, upper_some, 0)
+    for c in range(0, feat, 256):
+        v = dot(vm["up_own"][...], lown[:, c : c + 256]) + dot(vm["up_got"][...], lr[:, c : c + 256])
+        psl[:, :, :, c : c + 256] = v.reshape(psl.shape[0], 2, 8, 256)
 
     bases, at = [], 0
     for a, _ in sizes[1:]:
@@ -375,10 +368,16 @@
 
     loads["receive"].wait()
     field = near[...] + dot(inc0[...].reshape(own, feat), vm["receive"][...])
-    out_ref[...] = jnp.where(slot_of < cnt[...], field, 0.0).reshape(nx, ny, w)
+    out_ref[...] = jnp.where(slot_of < cnt[...], field, 0.0).astype(BF16).reshape(nx, ny, w)
 
     each(lambda d: copy(0, cs, cr, d, False).wait_send())
     each(lambda d: copy(1, ls, lr, d, False).wait_send())
+
+
+def hand_over(src, dst, sem):
+    copy = pltpu.make_async_copy(src, dst, sem)
+    copy.start()
+    copy.wait()
 
 
 EARLY = 11
@@ -410,8 +409,8 @@
         pltpu.VMEM((stack, feat), BF16),
         pltpu.VMEM((ROWS, feat), BF16),
         pltpu.VMEM((ROWS, feat), BF16),
-        pltpu.VMEM((nx + 4, ny + 8, feat), F32),
-        pltpu.VMEM((nx + 4, ny + 8, w), F32),
+        pltpu.VMEM((feat // 128, nx + 4, ny + 8, 128), F32),
+        pltpu.VMEM((w // 128, nx + 4, ny + 8, 128), F32),
         pltpu.VMEM((3, nx + 2, ny, w), BF16),
         pltpu.VMEM((6 * (nx // 2 + 2), 2, ny, feat), F32),
         pltpu.VMEM((consts["up_own"].shape[0] // 16, 2, 8, feat), F32),
@@ -423,9 +422,9 @@
         pltpu.SemaphoreType.DMA((2, 8)),
         pltpu.SemaphoreType.DMA((2, 8)),
     ]
-    return pl.pallas_call(
+    field = pl.pallas_call(
         functools.partial(body, ORDER, sizes),
-        out_shape=jax.ShapeDtypeStruct(currents.shape, F32),
+        out_shape=jax.ShapeDtypeStruct(currents.shape, BF16),
         in_specs=[pl.BlockSpec(memory_space=pl.ANY)] * len(args),
         out_specs=pl.BlockSpec(memory_space=pltpu.VMEM),
         scratch_shapes=scratch,
@@ -433,7 +432,14 @@
             collective_id=0, has_side_effects=True, vmem_limit_bytes=58 * 1024 * 1024
         ),
         cost_estimate=pl.CostEstimate(flops=3_000_000_000, bytes_accessed=12_000_000, transcendentals=0),
-    )(*args).astype(BF16)
+    )(*args)
+    return pl.pallas_call(
+        hand_over,
+        out_shape=jax.ShapeDtypeStruct(field.shape, field.dtype),
+        in_specs=[pl.BlockSpec(memory_space=pl.ANY)],
+        out_specs=pl.BlockSpec(memory_space=pl.ANY),
+        scratch_shapes=[pltpu.SemaphoreType.DMA],
+    )(field)
 
 
 def solution(mesh):

time: 31 us -> 34.7 us (1.12)
  Pallas kernels: 29 us -> 34.5 us
  other arithmetic: 1.78 us -> 0 us
    pallas_call x0 -> x1, Pallas kernels: none -> 9.05 us  [shards(): pl.pallas_call(hand_over, out_shape=jax.ShapeDtypeStruct(field.shape, fie...]
    pallas_call x1, Pallas kernels: 29 us -> 25.5 us  [shards(): pl.pallas_call(functools.partial(body, ORDER, sizes), out_shape=jax.Shape...]
    convert_element_type x1 -> x0, other arithmetic: 1.78 us -> none  [shards(): return pl.pallas_call(functools.partial(body, ORDER, sizes), out_shape=ja...]
where the time goes in v2:
time: 34.7 us; the launch traced here: 34.5 us
  Pallas kernels  34.5 us (99%)
    pallas_call x1, Pallas kernels, shards(): pl.pallas_call(functools.partial(body, ORDER, sizes), out_shape=jax.Shape...  25.5 us
    pallas_call x1, Pallas kernels, shards(): pl.pallas_call(hand_over, out_shape=jax.ShapeDtypeStruct(field.shape, fie...  9.05 us

profile of v2, /device:TPU:25, one launch (start us, length us, event | category | flops | bytes accessed | tf_op | source)
XLA Modules:
  0.0 34.5 jit_solution(8383945134877749568)
XLA Ops:
  0.0 25.5 %shard_map.199.src = bf16[16,16,512]{2,1,0:T(8,128)(2,1)} custom-call(s32[16,16]{1,0:T(8,128)} %refs_0_.1, bf16[256,16]{1,0:T(8,128)(2,1)} %constant.28.clone.refs_1_, bf16[256,16]{1,0:T(8,128)(2,1)} %constant.29.clone.refs_2_, bf16[16,16,512]{2,1,0:T(8,128)(2,1)} %refs_3_.1, bf16[192,256]{1,0:T(8,128)(2,1)} %constant.30.clone.refs_4_, ...), custom_call_target="tpu_custom_call" | custom-call | flops 3000000000 | bytes 12000000 | tf_op jit(solution)/shard_map/pallas_call | solution.py:425
  25.5 9.1 %shard_map.200 = bf16[16,16,512]{2,1,0:T(8,128)(2,1)} custom-call(bf16[16,16,512]{2,1,0:T(8,128)(2,1)} %shard_map.199.src), custom_call_target="tpu_custom_call" | custom-call | tf_op jit(solution)/shard_map/pallas_call | solution.py:436

commit v3 on v2

--- a/solution.py
+++ b/solution.py
@@ -265,7 +265,7 @@
                     v = e0[c, pl.ds(x, 1), 3 + s : 3 + s + ny, :]
                     if s == 3:
                         v = jnp.where(even16, v, e0[c, pl.ds(x, 1), 0:ny, :])
-                    ps0[pl.ds(n * pairs + k, 1), par, :, lanes] = v
+                    ps0[pl.ds(n * pairs + k, 1), par, :, lanes] = v.astype(BF16)
         return 0
 
     lax.fori_loop(0, pairs, shifted, 0)
@@ -294,6 +294,8 @@
             for a in range(2):
                 re = jnp.zeros((ni, rows, 128), F32)
                 im = jnp.zeros((ni, rows, 128), F32)
+                narrow = src.dtype == BF16
+                part, terms = None, 0
                 for e in range(6):
                     dx = e - 2 - a
                     for n, s in enumerate(SHIFTS):
@@ -307,8 +309,16 @@
                             ti = jnp.where(even, ti, translate[m, level : level + 1, il])
                         at = pl.ds(base + n * npair + e // 2 + h * ni, ni)
                         pr, pi = src[at, e % 2, :, rl], src[at, e % 2, :, il]
-                        re = re + (tr * pr - ti * pi)
-                        im = im + (tr * pi + ti * pr)
+                        if narrow:
+                            tr = jnp.broadcast_to(tr, (rows, 128)).astype(BF16)
+                            ti = jnp.broadcast_to(ti, (rows, 128)).astype(BF16)
+                        more = (tr * pr - ti * pi, tr * pi + ti * pr)
+                        part = more if part is None else (part[0] + more[0], part[1] + more[1])
+                        terms += 1
+                        if not narrow or terms % 3 == 0:
+                            re = re + part[0].astype(F32)
+                            im = im + part[1].astype(F32)
+                            part = None
                 at = pl.ds(h * ni, ni)
                 if lifted is not None:
                     tr = jnp.where(even, shift[level, 2 * a : 2 * a + 1, rl], shift[level, 2 * a + 1 : 2 * a + 2, rl])
@@ -374,10 +384,8 @@
     each(lambda d: copy(1, ls, lr, d, False).wait_send())
 
 
-def hand_over(src, dst, sem):
-    copy = pltpu.make_async_copy(src, dst, sem)
-    copy.start()
-    copy.wait()
+def hand_over(src, dst):
+    dst[...] = src[...]
 
 
 EARLY = 11
@@ -412,7 +420,7 @@
         pltpu.VMEM((feat // 128, nx + 4, ny + 8, 128), F32),
         pltpu.VMEM((w // 128, nx + 4, ny + 8, 128), F32),
         pltpu.VMEM((3, nx + 2, ny, w), BF16),
-        pltpu.VMEM((6 * (nx // 2 + 2), 2, ny, feat), F32),
+        pltpu.VMEM((6 * (nx // 2 + 2), 2, ny, feat), BF16),
         pltpu.VMEM((consts["up_own"].shape[0] // 16, 2, 8, feat), F32),
         level_buffer(0, F32), level_buffer(0, BF16), level_buffer(1, F32), level_buffer(2, F32), level_buffer(3, F32),
         level_buffer(0, F32), level_buffer(1, F32), level_buffer(2, F32),
@@ -436,9 +444,8 @@
     return pl.pallas_call(
         hand_over,
         out_shape=jax.ShapeDtypeStruct(field.shape, field.dtype),
-        in_specs=[pl.BlockSpec(memory_space=pl.ANY)],
-        out_specs=pl.BlockSpec(memory_space=pl.ANY),
-        scratch_shapes=[pltpu.SemaphoreType.DMA],
+        in_specs=[pl.BlockSpec(memory_space=pltpu.VMEM)],
+        out_specs=pl.BlockSpec(memory_space=pltpu.VMEM),
     )(field)
 
 

time: 34.7 us -> 25.8 us (0.74)
  Pallas kernels: 34.5 us -> 25.6 us
    pallas_call x1, Pallas kernels: 9.05 us -> 1.67 us  [shards(): pl.pallas_call(hand_over, out_shape=jax.ShapeDtypeStruct(field.shape, fie...]
    pallas_call x1, Pallas kernels: 25.5 us -> 24 us  [shards(): pl.pallas_call(functools.partial(body, ORDER, sizes), out_shape=jax.Shape...]
where the time goes in v3:
time: 25.8 us; the launch traced here: 25.6 us
  Pallas kernels  25.6 us (99%)
    pallas_call x1, Pallas kernels, shards(): pl.pallas_call(functools.partial(body, ORDER, sizes), out_shape=jax.Shape...  24 us
    pallas_call x1, Pallas kernels, shards(): pl.pallas_call(hand_over, out_shape=jax.ShapeDtypeStruct(field.shape, fie...  1.67 us

profile of v3, /device:TPU:25, one launch (start us, length us, event | category | flops | bytes accessed | tf_op | source)
XLA Modules:
  0.0 25.6 jit_solution(1242599015325602344)
XLA Ops:
  0.0 24.0 %shard_map.199.src = bf16[16,16,512]{2,1,0:T(8,128)(2,1)} custom-call(s32[16,16]{1,0:T(8,128)} %refs_0_.1, bf16[256,16]{1,0:T(8,128)(2,1)} %constant.28.clone.refs_1_, bf16[256,16]{1,0:T(8,128)(2,1)} %constant.29.clone.refs_2_, bf16[16,16,512]{2,1,0:T(8,128)(2,1)} %refs_3_.1, bf16[192,256]{1,0:T(8,128)(2,1)} %constant.30.clone.refs_4_, ...), custom_call_target="tpu_custom_call" | custom-call | flops 3000000000 | bytes 12000000 | tf_op jit(solution)/shard_map/pallas_call | solution.py:433
  24.0 1.7 %shard_map.200 = bf16[16,16,512]{2,1,0:T(8,128)(2,1)} custom-call(bf16[16,16,512]{2,1,0:T(8,128)(2,1)} %shard_map.199.src), custom_call_target="tpu_custom_call" | custom-call | tf_op jit(solution)/shard_map/pallas_call | solution.py:444

commit v4 on v3

--- a/solution.py
+++ b/solution.py
@@ -274,13 +274,16 @@
         for c in range(w // 128):
             ns[n, :, :, c * 128 : c * 128 + 128] = f0[c, 1 : nx + 3, 2 + n : 2 + n + ny, :].astype(BF16)
     loads["near_blocks"].wait()
-    views = [ns[k % 3, k // 3 : k // 3 + nx].reshape(own, w) for k in range(9)]
-    near[...] = dot(jnp.concatenate(views, axis=1), vm["near_blocks"][...].reshape(9 * w, w))
+
+    def near_part(n):
+        columns = pl.ds(pl.multiple_of(n * (w // 2), w // 2), w // 2)
+        views = [ns[k % 3, k // 3 : k // 3 + nx].reshape(own, w) for k in range(9)]
+        near[:, columns] = dot(jnp.concatenate(views, axis=1), vm["near_blocks"][:, :, columns].reshape(9 * w, w // 2))
 
     loads["translate"].wait()
     translate = vm["translate"]
 
-    def far(level, src, base, inc, lifted):
+    def far(level, src, base, inc, lifted, beside=None):
         rows = src.shape[2]
         n_pairs = sizes[level][0] // 2
         npair = n_pairs + 2
@@ -288,7 +291,16 @@
         even = (lax.broadcasted_iota(jnp.int32, (rows, 128), 0) % 2) == 0
 
         def step(it, _):
-            t, h = lax.rem(it, tiles), lax.div(it, tiles)
+            if beside is None:
+                piece(lax.rem(it, tiles), lax.div(it, tiles))
+            else:
+                beside(it)
+                for k in range(tiles // 2):
+                    for h in range(n_pairs // ni):
+                        piece(it * (tiles // 2) + k, h)
+            return 0
+
+        def piece(t, h):
             rl = pl.ds(pl.multiple_of(t * 128, 128), 128)
             il = pl.ds(pl.multiple_of(half + t * 128, 128), 128)
             for a in range(2):
@@ -328,9 +340,8 @@
                     im = im + (tr * pi - ti * pr)
                 inc[at, a, :, rl] = re.astype(inc.dtype)
                 inc[at, a, :, il] = im.astype(inc.dtype)
-            return 0
-
-        lax.fori_loop(0, tiles * (n_pairs // ni), step, 0)
+
+        lax.fori_loop(0, tiles * (n_pairs // ni) if beside is None else 2, step, 0)
 
     def lift(name, inc, dst):
         loads[name].wait()
@@ -341,7 +352,7 @@
         low = (rest - mid.astype(F32)).astype(BF16)
         dst[...] = dot(vm[name][...], jnp.concatenate([hi, mid, low], axis=0)).reshape(dst.shape)
 
-    far(0, ps0, 0, far0, None)
+    far(0, ps0, 0, far0, None, near_part)
 
     loads["up_own"].wait()
     loads["up_got"].wait()

time: 25.8 us -> 25.1 us (0.973)
  Pallas kernels: 25.6 us -> 24.9 us
    pallas_call x1, Pallas kernels: 24 us -> 23.3 us  [shards(): pl.pallas_call(functools.partial(body, ORDER, sizes), out_shape=jax.Shape...]
where the time goes in v4:
time: 25.1 us; the launch traced here: 24.9 us
  Pallas kernels  24.9 us (99%)
    pallas_call x1, Pallas kernels, shards(): pl.pallas_call(functools.partial(body, ORDER, sizes), out_shape=jax.Shape...  23.3 us
    pallas_call x1, Pallas kernels, shards(): pl.pallas_call(hand_over, out_shape=jax.ShapeDtypeStruct(field.shape, fie...  1.67 us

profile of v4, /device:TPU:25, one launch (start us, length us, event | category | flops | bytes accessed | tf_op | source)
XLA Modules:
  0.0 24.9 jit_solution(14235085812118794332)
XLA Ops:
  0.0 23.3 %shard_map.199.src = bf16[16,16,512]{2,1,0:T(8,128)(2,1)} custom-call(s32[16,16]{1,0:T(8,128)} %refs_0_.1, bf16[256,16]{1,0:T(8,128)(2,1)} %constant.28.clone.refs_1_, bf16[256,16]{1,0:T(8,128)(2,1)} %constant.29.clone.refs_2_, bf16[16,16,512]{2,1,0:T(8,128)(2,1)} %refs_3_.1, bf16[192,256]{1,0:T(8,128)(2,1)} %constant.30.clone.refs_4_, ...), custom_call_target="tpu_custom_call" | custom-call | flops 3000000000 | bytes 12000000 | tf_op jit(solution)/shard_map/pallas_call | solution.py:444
  23.3 1.7 %shard_map.200 = bf16[16,16,512]{2,1,0:T(8,128)(2,1)} custom-call(bf16[16,16,512]{2,1,0:T(8,128)(2,1)} %shard_map.199.src), custom_call_target="tpu_custom_call" | custom-call | tf_op jit(solution)/shard_map/pallas_call | solution.py:455

commit v5 on v4

--- a/solution.py
+++ b/solution.py
@@ -341,7 +341,7 @@
                 inc[at, a, :, rl] = re.astype(inc.dtype)
                 inc[at, a, :, il] = im.astype(inc.dtype)
 
-        lax.fori_loop(0, tiles * (n_pairs // ni) if beside is None else 2, step, 0)
+        lax.fori_loop(0, tiles * (n_pairs // ni) if beside is None else 2, step, 0, unroll=beside is None)
 
     def lift(name, inc, dst):
         loads[name].wait()
@@ -385,7 +385,7 @@
             inc0[:, a, :, il] = (far0[:, a, :, il] + (tr * pi - ti * pr)).astype(BF16)
         return 0
 
-    lax.fori_loop(0, tiles, from_parents, 0)
+    lax.fori_loop(0, tiles, from_parents, 0, unroll=True)
 
     loads["receive"].wait()
     field = near[...] + dot(inc0[...].reshape(own, feat), vm["receive"][...])

time: 25.1 us -> 23.6 us (0.940)
  Pallas kernels: 24.9 us -> 23.4 us
    pallas_call x1, Pallas kernels: 23.3 us -> 21.7 us  [shards(): pl.pallas_call(functools.partial(body, ORDER, sizes), out_shape=jax.Shape...]
where the time goes in v5:
time: 23.6 us; the launch traced here: 23.4 us
  Pallas kernels  23.4 us (99%)
    pallas_call x1, Pallas kernels, shards(): pl.pallas_call(functools.partial(body, ORDER, sizes), out_shape=jax.Shape...  21.7 us
    pallas_call x1, Pallas kernels, shards(): pl.pallas_call(hand_over, out_shape=jax.ShapeDtypeStruct(field.shape, fie...  1.67 us

profile of v5, /device:TPU:25, one launch (start us, length us, event | category | flops | bytes accessed | tf_op | source)
XLA Modules:
  0.0 23.4 jit_solution(828854330866131328)
XLA Ops:
  0.0 21.7 %shard_map.199.src = bf16[16,16,512]{2,1,0:T(8,128)(2,1)} custom-call(s32[16,16]{1,0:T(8,128)} %refs_0_.1, bf16[256,16]{1,0:T(8,128)(2,1)} %constant.28.clone.refs_1_, bf16[256,16]{1,0:T(8,128)(2,1)} %constant.29.clone.refs_2_, bf16[16,16,512]{2,1,0:T(8,128)(2,1)} %refs_3_.1, bf16[192,256]{1,0:T(8,128)(2,1)} %constant.30.clone.refs_4_, ...), custom_call_target="tpu_custom_call" | custom-call | flops 3000000000 | bytes 12000000 | tf_op jit(solution)/shard_map/pallas_call | solution.py:444
  21.7 1.7 %shard_map.200 = bf16[16,16,512]{2,1,0:T(8,128)(2,1)} custom-call(bf16[16,16,512]{2,1,0:T(8,128)(2,1)} %shard_map.199.src), custom_call_target="tpu_custom_call" | custom-call | tf_op jit(solution)/shard_map/pallas_call | solution.py:455
